TPU v7x, 32 devices: a whole 2x2x4 slice. The times are simulated.
32 devices in a mesh: wide: 8 (over z, x), narrow: 4 (over y, core).
Axes of the slice: x: 2, y: 2, z: 4, core: 2. Of those that a mesh axis runs over, the one named last changes fastest.
Arguments:
- tokens: bfloat16 [32768, 1024], P(('wide', 'narrow')), may hold values from -6 to 6
- attn_gain: bfloat16 [1024], P(('wide', 'narrow')), may hold values from 0.099609375 to 1.8984375
- attn_shift: bfloat16 [1024], P(('wide', 'narrow')), may hold values from -3 to 3
- qkv_weight: bfloat16 [1024, 3072], P(('wide', 'narrow')), may hold values from -0.1875 to 0.1875
- qv_bias: bfloat16 [2048], P(('wide', 'narrow')), may hold values from -3 to 3
- out_weight: bfloat16 [1024, 1024], P(('wide', 'narrow')), may hold values from -3 to 3
- out_bias: bfloat16 [1024], P(('wide', 'narrow')), may hold values from -3 to 3
- mlp_gain: bfloat16 [1024], P(('wide', 'narrow')), may hold values from 0.099609375 to 1.8984375
- mlp_shift: bfloat16 [1024], P(('wide', 'narrow')), may hold values from -3 to 3
- up_weight: bfloat16 [1024, 4096], P(('wide', 'narrow')), may hold values from -0.1875 to 0.1875
- up_bias: bfloat16 [4096], P(('wide', 'narrow')), may hold values from -3 to 3
- down_weight: bfloat16 [4096, 1024], P(('wide', 'narrow')), may hold values from -0.125 to 0.125
- down_bias: bfloat16 [1024], P(('wide', 'narrow')), may hold values from -3 to 3
- cotangent: bfloat16 [32768, 1024], P(('wide', 'narrow')), may hold values from -6 to 6
Outputs:
- output: bfloat16 [32768, 1024], P(('wide', 'narrow'))
- grad_tokens: bfloat16 [32768, 1024], P(('wide', 'narrow'))
- grad_attn_gain: float32 [1024], P(('wide', 'narrow'))
- grad_attn_shift: float32 [1024], P(('wide', 'narrow'))
- grad_qkv_weight: float32 [1024, 3072], P(('wide', 'narrow'))
- grad_qv_bias: float32 [2048], P(('wide', 'narrow'))
- grad_out_weight: float32 [1024, 1024], P(('wide', 'narrow'))
- grad_out_bias: float32 [1024], P(('wide', 'narrow'))
- grad_mlp_gain: float32 [1024], P(('wide', 'narrow'))
- grad_mlp_shift: float32 [1024], P(('wide', 'narrow'))
- grad_up_weight: float32 [1024, 4096], P(('wide', 'narrow'))
- grad_up_bias: float32 [4096], P(('wide', 'narrow'))
- grad_down_weight: float32 [4096, 1024], P(('wide', 'narrow'))
- grad_down_bias: float32 [1024], P(('wide', 'narrow'))
All inputs are finite; a program needn't handle non-finite values.
Results may differ from a plain program's by a relative error of at most 0.012.
The roundings to bfloat16 on the way count: a program that leaves them out, or rounds other values in their place, can miss the bound.
Values may be sent and summed in bfloat16 or wider, within the bound.
A program may use at most 320 MiB of HBM per device.

v0:
```python
import jax
import jax.numpy as jnp
from jax import lax
from jax.sharding import PartitionSpec as P

H = 16
HD = 64


epsilon = 1e-05


def layer_norm(values_in, gain_vec, bias_vec):
    row_mean = jnp.mean(values_in, axis=-1, keepdims=True)
    centred = values_in - row_mean
    spread = jnp.mean(centred * centred, axis=-1, keepdims=True)
    return centred * lax.rsqrt(spread + epsilon) * gain_vec + bias_vec


def gelu_exact(values_in):
    return jax.nn.gelu(values_in, approximate=False)


def norm_backward(values_in, gain_vec, incoming):
    zero_shift = jnp.zeros_like(gain_vec)
    unused, pull_back = jax.vjp(layer_norm, values_in, gain_vec, zero_shift)
    return pull_back(incoming)


def local(
    tokens,
    attn_gain,
    attn_shift,
    qkv_weight,
    qv_bias,
    out_weight,
    out_bias,
    mlp_gain,
    mlp_shift,
    up_weight,
    up_bias,
    down_weight,
    down_bias,
    cotangent,
):
    length, model_width = tokens.shape
    score_scale = HD ** (-0.5)
    gain_a, shift_a, qkv_full, qv_full, out_full, out_bias_full = (
        lax.all_gather(attn_gain, ("wide", "narrow"), axis=0, tiled=True),
        lax.all_gather(attn_shift, ("wide", "narrow"), axis=0, tiled=True),
        lax.all_gather(qkv_weight, ("wide", "narrow"), axis=0, tiled=True),
        lax.all_gather(qv_bias, ("wide", "narrow"), axis=0, tiled=True),
        lax.all_gather(out_weight, ("wide", "narrow"), axis=0, tiled=True),
        lax.all_gather(out_bias, ("wide", "narrow"), axis=0, tiled=True),
    )
    inputs = tokens.astype(jnp.float32)
    act_a = layer_norm(inputs, gain_a.astype(jnp.float32), shift_a.astype(jnp.float32)).astype(
        jnp.bfloat16
    )
    bias_full = jnp.concatenate(
        [qv_full[:model_width], jnp.zeros((model_width,), jnp.bfloat16), qv_full[model_width:]]
    ).astype(jnp.float32)
    projected = (jnp.dot(act_a, qkv_full, preferred_element_type=jnp.float32) + bias_full).astype(
        jnp.bfloat16
    )
    query_rows = projected[:, :model_width].reshape(length, H, HD)
    key_rows = projected[:, model_width : 2 * model_width].reshape(length, H, HD)
    value_rows = projected[:, 2 * model_width :].reshape(length, H, HD)
    block_rows = min(512, length)
    block_count = length // block_rows
    query_blocks = query_rows.reshape(block_count, block_rows, H, HD)

    def attend_block(query_block):
        scores = (
            jnp.einsum("qhe,khe->hqk", query_block, key_rows, preferred_element_type=jnp.float32)
            * score_scale
        )
        row_max = jnp.max(scores, axis=-1, keepdims=True)
        exp_scores = jnp.exp(scores - row_max)
        denominator = jnp.sum(exp_scores, axis=-1, keepdims=True)
        low_probs = (exp_scores / denominator).astype(jnp.bfloat16)
        mixed_block = jnp.einsum(
            "hqk,khe->qhe", low_probs, value_rows, preferred_element_type=jnp.float32
        )
        return (mixed_block, (row_max + jnp.log(denominator))[..., 0])

    mixed_blocks, log_sums = lax.map(attend_block, query_blocks)
    mixed = mixed_blocks.reshape(length, model_width).astype(jnp.bfloat16)
    hidden = (
        inputs
        + jnp.dot(mixed, out_full, preferred_element_type=jnp.float32)
        + out_bias_full.astype(jnp.float32)
    )
    gain_b, shift_b, up_full, up_bias_full, down_full, down_bias_full = (
        lax.all_gather(mlp_gain, ("wide", "narrow"), axis=0, tiled=True),
        lax.all_gather(mlp_shift, ("wide", "narrow"), axis=0, tiled=True),
        lax.all_gather(up_weight, ("wide", "narrow"), axis=0, tiled=True),
        lax.all_gather(up_bias, ("wide", "narrow"), axis=0, tiled=True),
        lax.all_gather(down_weight, ("wide", "narrow"), axis=0, tiled=True),
        lax.all_gather(down_bias, ("wide", "narrow"), axis=0, tiled=True),
    )
    act_b = layer_norm(hidden, gain_b.astype(jnp.float32), shift_b.astype(jnp.float32)).astype(
        jnp.bfloat16
    )
    pre_up = jnp.dot(act_b, up_full, preferred_element_type=jnp.float32) + up_bias_full.astype(
        jnp.float32
    )
    act_c = gelu_exact(pre_up).astype(jnp.bfloat16)
    output = (
        hidden
        + jnp.dot(act_c, down_full, preferred_element_type=jnp.float32)
        + down_bias_full.astype(jnp.float32)
    ).astype(jnp.bfloat16)
    gain_b_back, up_back, down_back = (
        lax.all_gather(mlp_gain, ("wide", "narrow"), axis=0, tiled=True),
        lax.all_gather(up_weight, ("wide", "narrow"), axis=0, tiled=True),
        lax.all_gather(down_weight, ("wide", "narrow"), axis=0, tiled=True),
    )
    grad_y = cotangent.astype(jnp.float32)
    grad_down_weight = jnp.einsum("sf,sd->fd", act_c, cotangent, preferred_element_type=jnp.float32)
    grad_down_bias = jnp.sum(cotangent.astype(jnp.float32), axis=0)
    grad_act = jnp.einsum("sd,fd->sf", cotangent, down_back, preferred_element_type=jnp.float32)
    unused_gelu, gelu_pull = jax.vjp(gelu_exact, pre_up)
    grad_pre = gelu_pull(grad_act)[0].astype(jnp.bfloat16)
    grad_up_weight = jnp.einsum("sd,sf->df", act_b, grad_pre, preferred_element_type=jnp.float32)
    grad_up_bias = jnp.sum(grad_pre.astype(jnp.float32), axis=0)
    grad_act_b = jnp.einsum("sf,df->sd", grad_pre, up_back, preferred_element_type=jnp.float32)
    hidden_part, grad_mlp_gain, grad_mlp_shift = norm_backward(
        hidden, gain_b_back.astype(jnp.float32), grad_act_b
    )
    grad_hidden = grad_y + hidden_part
    mlp_sums = (
        lax.psum_scatter(grad_mlp_gain, ("wide", "narrow"), scatter_dimension=0, tiled=True),
        lax.psum_scatter(grad_mlp_shift, ("wide", "narrow"), scatter_dimension=0, tiled=True),
        lax.psum_scatter(grad_up_weight, ("wide", "narrow"), scatter_dimension=0, tiled=True),
        lax.psum_scatter(grad_up_bias, ("wide", "narrow"), scatter_dimension=0, tiled=True),
        lax.psum_scatter(grad_down_weight, ("wide", "narrow"), scatter_dimension=0, tiled=True),
        lax.psum_scatter(grad_down_bias, ("wide", "narrow"), scatter_dimension=0, tiled=True),
    )
    gain_a_back, qkv_back, out_back = (
        lax.all_gather(attn_gain, ("wide", "narrow"), axis=0, tiled=True),
        lax.all_gather(qkv_weight, ("wide", "narrow"), axis=0, tiled=True),
        lax.all_gather(out_weight, ("wide", "narrow"), axis=0, tiled=True),
    )
    grad_branch = grad_hidden.astype(jnp.bfloat16)
    grad_out_weight = jnp.einsum(
        "sa,sd->ad", mixed, grad_branch, preferred_element_type=jnp.float32
    )
    grad_out_bias = jnp.sum(grad_branch.astype(jnp.float32), axis=0)
    grad_mixed = jnp.einsum(
        "sd,ad->sa", grad_branch, out_back, preferred_element_type=jnp.float32
    ).astype(jnp.bfloat16)
    grad_blocks = grad_mixed.reshape(block_count, block_rows, H, HD)

    def back_block(carry, block_inputs):
        key_total, value_total = carry
        query_block, grad_block, log_block = block_inputs
        scores = (
            jnp.einsum("qhe,khe->hqk", query_block, key_rows, preferred_element_type=jnp.float32)
            * score_scale
        )
        attn_probs = jnp.exp(scores - log_block[..., None])
        grad_probs = jnp.einsum(
            "qhe,khe->hqk", grad_block, value_rows, preferred_element_type=jnp.float32
        )
        row_delta = jnp.sum(grad_probs * attn_probs, axis=-1, keepdims=True)
        grad_scores = (attn_probs * (grad_probs - row_delta)).astype(jnp.bfloat16)
        low_probs = attn_probs.astype(jnp.bfloat16)
        value_total = value_total + jnp.einsum(
            "hqk,qhe->khe", low_probs, grad_block, preferred_element_type=jnp.float32
        )
        key_total = (
            key_total
            + jnp.einsum(
                "hqk,qhe->khe", grad_scores, query_block, preferred_element_type=jnp.float32
            )
            * score_scale
        )
        grad_query = (
            jnp.einsum("hqk,khe->qhe", grad_scores, key_rows, preferred_element_type=jnp.float32)
            * score_scale
        )
        return ((key_total, value_total), grad_query)

    zero_heads = jnp.zeros((length, H, HD), jnp.float32)
    (grad_key, grad_value), grad_query = lax.scan(
        back_block, (zero_heads, zero_heads), (query_blocks, grad_blocks, log_sums)
    )
    grad_projected = jnp.concatenate(
        [
            grad_query.reshape(length, model_width),
            grad_key.reshape(length, model_width),
            grad_value.reshape(length, model_width),
        ],
        axis=1,
    ).astype(jnp.bfloat16)
    grad_qkv_weight = jnp.einsum(
        "sa,sb->ab", act_a, grad_projected, preferred_element_type=jnp.float32
    )
    column_sums = jnp.sum(grad_projected.astype(jnp.float32), axis=0)
    grad_qv_bias = jnp.concatenate([column_sums[:model_width], column_sums[2 * model_width :]])
    grad_act_a = jnp.einsum(
        "sb,ab->sa", grad_projected, qkv_back, preferred_element_type=jnp.float32
    )
    input_part, grad_attn_gain, grad_attn_shift = norm_backward(
        inputs, gain_a_back.astype(jnp.float32), grad_act_a
    )
    grad_tokens = (grad_hidden + input_part).astype(jnp.bfloat16)
    attn_sums = (
        lax.psum_scatter(grad_attn_gain, ("wide", "narrow"), scatter_dimension=0, tiled=True),
        lax.psum_scatter(grad_attn_shift, ("wide", "narrow"), scatter_dimension=0, tiled=True),
        lax.psum_scatter(grad_qkv_weight, ("wide", "narrow"), scatter_dimension=0, tiled=True),
        lax.psum_scatter(grad_qv_bias, ("wide", "narrow"), scatter_dimension=0, tiled=True),
        lax.psum_scatter(grad_out_weight, ("wide", "narrow"), scatter_dimension=0, tiled=True),
        lax.psum_scatter(grad_out_bias, ("wide", "narrow"), scatter_dimension=0, tiled=True),
    )
    return (
        output,
        grad_tokens,
        attn_sums[0],
        attn_sums[1],
        attn_sums[2],
        attn_sums[3],
        attn_sums[4],
        attn_sums[5],
        mlp_sums[0],
        mlp_sums[1],
        mlp_sums[2],
        mlp_sums[3],
        mlp_sums[4],
        mlp_sums[5],
    )


def solution(mesh):
    placed = (
        P(("wide", "narrow"), None),
        P(("wide", "narrow")),
        P(("wide", "narrow")),
        P(("wide", "narrow"), None),
        P(("wide", "narrow")),
        P(("wide", "narrow"), None),
        P(("wide", "narrow")),
        P(("wide", "narrow")),
        P(("wide", "narrow")),
        P(("wide", "narrow"), None),
        P(("wide", "narrow")),
        P(("wide", "narrow"), None),
        P(("wide", "narrow")),
        P(("wide", "narrow"), None),
    )
    return jax.shard_map(
        local,
        mesh=mesh,
        in_specs=placed,
        out_specs=(
            P(("wide", "narrow"), None),
            P(("wide", "narrow"), None),
            P(("wide", "narrow")),
            P(("wide", "narrow")),
            P(("wide", "narrow"), None),
            P(("wide", "narrow")),
            P(("wide", "narrow"), None),
            P(("wide", "narrow")),
            P(("wide", "narrow")),
            P(("wide", "narrow")),
            P(("wide", "narrow"), None),
            P(("wide", "narrow")),
            P(("wide", "narrow"), None),
            P(("wide", "narrow")),
        ),
        check_vma=False,
    )
```

profile of v0, /device:TPU:0, one launch (start us, length us, event | category | flops | bytes accessed | tf_op | source)
XLA Modules:
  0.0 1168.7 jit_solution(16688019018912999818)
XLA Ops:
  15.9 42.4 %all-reduce.16 = (bf16[1024]{0:T(1024)(128)(2,1)S(1)}, bf16[2048]{0:T(1024)(128)(2,1)S(1)}, bf16[1024]{0:T(1024)(128)(2,1)S(1)}, bf16[1024]{0:T(1024)(128)(2,1)S...) all-reduce(bf16[1024]{0:T(1024)(128)(2,1)S(1)} %dynamic-update-slic, ...), channel_id=1, replica_groups=mesh['wide'=8,'narrow'=4] {'wide','narrow'}, use_global_device_ids=true, to_apply=%add.3 | all-reduce | flops 8192 | bytes 32768
  60.2 40.7 %all-gather = bf16[32,1,128]{2,1,0:T(2,128)(2,1)S(1)} all-gather(bf16[1,1,128]{2,1,0:T(2,128)(2,1)} %bitcast.125), channel_id=1, replica_groups=mesh['wide'=8,'narrow'=4] {'wide','narrow'}, dimensions={0}, use_global_device_ids=true | all-gather | bytes 8448 | tf_op jit(solution)/shard_map/all_gather | solution.py:98
  110.0 10.3 add_convert_fusion.1
  140.9 93.9 %while.27 = (s32[]{:T(128)}, bf16[2,512,16,64]{1,3,2,0:T(8,128)(2,1)S(1)}, f32[2,16,512]{2,1,0:T(8,128)S(1)}, bf16[2,512,16,64]{1,3,2,0:T(8,128)(2,1)}, bf16[102...) while((s32[]{:T(128)}, bf16[2,512,16,64]{1,3,2,0:T(8,128)(2,1)S(1)}, ...), condition=%wide.region_5.6_spmd, body=%wide.region_2.5_spmd.sunk | while | flops 2222972928 | bytes 108265568 | solution.py:87
  141.1 17.9 %multiply_reduce_fusion.7 = (f32[16,512]{1,0:T(8,128)S(1)}, f32[16,512,1024]{2,1,0:T(8,128)}) fusion(bf16[1024,16,64]{0,2,1:T(8,128)(2,1)} %get-tuple-element.411, bf16[2,512,16,64]{1,3,2,0:T(8,128)(2,1)} %get-tuple-element.410, s32[]{:T(128)S(6)} %copy.100), kind=kOutput, calls=%fused_computation.2.clone.1 | convolution fusion | flops 1090510848 | bytes 36732932 | tf_op jit(solution)/shard_map/while/body/eval_jaxpr/qhe,khe->hqk/dot_general | solution.py:75
  159.0 14.2 %fusion.108 = f32[16,512]{1,0:T(8,128)S(1)} fusion(f32[16,512,1024]{2,1,0:T(8,128)} %get-tuple-element.380, f32[16,512]{1,0:T(8,128)S(1)} %get-tuple-element.381), kind=kLoop, calls=%fused_computation.3.clone.1 | loop fusion | flops 25157632 | bytes 33619968 | tf_op jit(solution)/shard_map/while/body/eval_jaxpr/reduce_sum | solution.py:80
  173.2 14.3 %bitcast_dynamic-update-slice_fusion.6 = bf16[2,512,16,64]{1,3,2,0:T(8,128)(2,1)S(1)} fusion(bf16[2,512,16,64]{1,3,2,0:T(8,128)(2,1)S(1)} %get-tuple-element.401, s32[]{:T(128)S(6)} %copy.100, bf16[1024,16,64]{0,2,1:T(8,128)(2,1)} %get-tuple-element.412, f32[16,512,1024]{2,1,0:T(8,128)} %get-tuple-element.380, f32[16,512]{1,0:T(8,128)S(1)} %fusion.108, ...), kind=kOutput, calls=%fused_computation.5.clone.1 | convolution fusion | flops 1107296256 | bytes 37814276 | tf_op jit(solution)/shard_map/while/body/eval_jaxpr/hqk,khe->qhe/dot_general | solution.py:82
  187.6 17.8 %multiply_reduce_fusion.7 = (f32[16,512]{1,0:T(8,128)S(1)}, f32[16,512,1024]{2,1,0:T(8,128)}) fusion(bf16[1024,16,64]{0,2,1:T(8,128)(2,1)} %get-tuple-element.411, bf16[2,512,16,64]{1,3,2,0:T(8,128)(2,1)} %get-tuple-element.410, s32[]{:T(128)S(6)} %copy.100), kind=kOutput, calls=%fused_computation.2.clone.1 | convolution fusion | flops 1090510848 | bytes 36732932 | tf_op jit(solution)/shard_map/while/body/eval_jaxpr/qhe,khe->hqk/dot_general | solution.py:75
  205.4 14.5 %fusion.108 = f32[16,512]{1,0:T(8,128)S(1)} fusion(f32[16,512,1024]{2,1,0:T(8,128)} %get-tuple-element.380, f32[16,512]{1,0:T(8,128)S(1)} %get-tuple-element.381), kind=kLoop, calls=%fused_computation.3.clone.1 | loop fusion | flops 25157632 | bytes 33619968 | tf_op jit(solution)/shard_map/while/body/eval_jaxpr/reduce_sum | solution.py:80
  219.8 14.5 %bitcast_dynamic-update-slice_fusion.6 = bf16[2,512,16,64]{1,3,2,0:T(8,128)(2,1)S(1)} fusion(bf16[2,512,16,64]{1,3,2,0:T(8,128)(2,1)S(1)} %get-tuple-element.401, s32[]{:T(128)S(6)} %copy.100, bf16[1024,16,64]{0,2,1:T(8,128)(2,1)} %get-tuple-element.412, f32[16,512,1024]{2,1,0:T(8,128)} %get-tuple-element.380, f32[16,512]{1,0:T(8,128)S(1)} %fusion.108, ...), kind=kOutput, calls=%fused_computation.5.clone.1 | convolution fusion | flops 1107296256 | bytes 37814276 | tf_op jit(solution)/shard_map/while/body/eval_jaxpr/hqk,khe->qhe/dot_general | solution.py:82
  250.2 17.0 %fusion.56 = f32[1024,4096]{1,0:T(8,128)} fusion(bf16[1024,4096]{1,0:T(8,128)(2,1)} %all-gather.10.cloned.1.call-done, f32[1024,1024]{0,1:T(8,128)} %copy-done.9, f32[1024]{0:T(1024)S(1)} %copy-done.51, f32[1024]{0:T(1024)S(1)} %copy-done.37, f32[1024]{0:T(1024)S(1)} %fusion.50, f32[1024]{0:T(1024)S(1)} %broadcast_multiply_fusion), kind=kOutput, calls=%fused_computation.103 | convolution fusion | flops 8595177472 | bytes 29376512 | tf_op jit(solution)/shard_map/dot_general | solution.py:105
  267.2 32.3 %all-gather.12.cloned.1.call-done = bf16[4096,1024]{1,0:T(8,128)(2,1)} async-done(((bf16[128,1024]{1,0:T(8,128)(2,1)}), bf16[4096,1024]{1,0:T(8,128)(2,1)}) %all-gather.12.cloned.1.call-update) | async-done | bytes 8388624 | tf_op jit(solution)/shard_map/all_gather | solution.py:99
  299.5 51.7 %convert_reduce_fusion = (f32[4096]{0:T(1024)}, bf16[1024,4096]{1,0:T(8,128)(2,1)S(1)}, f32[1024,4096]{1,0:T(8,128)}) fusion(f32[1024,4096]{1,0:T(8,128)} %fusion.56, f32[4096]{0:T(1024)S(1)} %bitcast.123, bf16[1024,1024]{1,0:T(8,128)(2,1)S(1)} %copy-done.19, bf16[4096,1024]{1,0:T(8,128)(2,1)} %all-gather.12.cloned.1.call-done), kind=kOutput, calls=%fused_computation.40 | convolution fusion | flops 8904503296 | bytes 52461568 | tf_op jit(solution)/shard_map/sd,fd->sf/dot_general | solution.py:122
  351.2 11.1 fusion.65
  401.2 212.1 %while.28 = (s32[]{:T(128)}, f32[1024,16,64]{0,2,1:T(8,128)}, f32[1024,16,64]{0,2,1:T(8,128)}, bf16[2,512,16,64]{1,3,2,0:T(8,128)(2,1)}, bf16[2,512,16,64]{1,3,2...) while((s32[]{:T(128)}, f32[1024,16,64]{0,2,1:T(8,128)}, ...), condition=%wide.region_12.13_spmd.clone, body=%wide.region_10.12_spmd.clone.sunk | while | flops 5475131392 | bytes 348356800 | solution.py:186
  401.6 17.7 %fusion.118 = f32[16,512,1024]{2,1,0:T(8,128)} fusion(bf16[1024,16,64]{0,2,1:T(8,128)(2,1)} %get-tuple-element.441, bf16[2,512,16,64]{1,3,2,0:T(8,128)(2,1)} %get-tuple-element.440, s32[]{:T(128)S(6)} %copy.110), kind=kOutput, calls=%fused_computation.26.clone.1 | convolution fusion | flops 1073741824 | bytes 36700164 | tf_op jit(solution)/shard_map/while/body/eval_jaxpr/qhe,khe->hqk/dot_general | solution.py:159
  419.3 16.6 %bitcast_add_fusion.5 = f32[1024,16,64]{0,2,1:T(8,128)} fusion(f32[1024,16,64]{0,2,1:T(8,128)} %get-tuple-element.427, f32[16,512,1024]{2,1,0:T(8,128)} %fusion.118, f32[16,512]{1,0:T(8,128)S(1)} %dynamic-slice_bitcast_fusion.2, pred[]{:T(512)S(6)} %compare.3, bf16[2,512,16,64]{1,3,2,0:T(8,128)(2,1)} %get-tuple-element.443, s32[]{:T(128)S(6)} %copy.110), kind=kOutput, calls=%fused_computation.19.clone.1 | convolution fusion | flops 1101004800 | bytes 43024388 | tf_op jit(solution)/shard_map/while/body/eval_jaxpr/hqk,qhe->khe/dot_general | solution.py:169
  435.9 24.3 %multiply_reduce_fusion.8 = (f32[16,512]{1,0:T(8,128)S(1)}, f32[16,512,1024]{2,1,0:T(8,128)}) fusion(f32[16,512,1024]{2,1,0:T(8,128)} %fusion.118, f32[16,512]{1,0:T(8,128)S(1)} %dynamic-slice_bitcast_fusion.2, bf16[1024,16,64]{0,2,1:T(8,128)(2,1)} %get-tuple-element.444, bf16[2,512,16,64]{1,3,2,0:T(8,128)(2,1)} %get-tuple-element.443, s32[]{:T(128)S(6)} %copy.110), kind=kOutput, calls=%fused_computation.13.clone.1 | convolution fusion | flops 1107288064 | bytes 70320128 | tf_op jit(solution)/shard_map/while/body/eval_jaxpr/qhe,khe->hqk/dot_general | solution.py:163
  460.2 28.1 %multiply_convert_fusion.3 = bf16[16,512,1024]{2,1,0:T(8,128)(2,1)} fusion(f32[16,512,1024]{2,1,0:T(8,128)} %get-tuple-element.391, f32[16,512,1024]{2,1,0:T(8,128)} %fusion.118, f32[16,512]{1,0:T(8,128)S(1)} %get-tuple-element.392, f32[16,512]{1,0:T(8,128)S(1)} %dynamic-slice_bitcast_fusion.2), kind=kLoop, calls=%fused_computation.12.clone.1 | loop fusion | flops 41943040 | bytes 83951616 | tf_op jit(solution)/shard_map/while/body/eval_jaxpr/convert_element_type | solution.py:167
  506.5 17.7 %fusion.118 = f32[16,512,1024]{2,1,0:T(8,128)} fusion(bf16[1024,16,64]{0,2,1:T(8,128)(2,1)} %get-tuple-element.441, bf16[2,512,16,64]{1,3,2,0:T(8,128)(2,1)} %get-tuple-element.440, s32[]{:T(128)S(6)} %copy.110), kind=kOutput, calls=%fused_computation.26.clone.1 | convolution fusion | flops 1073741824 | bytes 36700164 | tf_op jit(solution)/shard_map/while/body/eval_jaxpr/qhe,khe->hqk/dot_general | solution.py:159
  524.2 17.7 %bitcast_add_fusion.5 = f32[1024,16,64]{0,2,1:T(8,128)} fusion(f32[1024,16,64]{0,2,1:T(8,128)} %get-tuple-element.427, f32[16,512,1024]{2,1,0:T(8,128)} %fusion.118, f32[16,512]{1,0:T(8,128)S(1)} %dynamic-slice_bitcast_fusion.2, pred[]{:T(512)S(6)} %compare.3, bf16[2,512,16,64]{1,3,2,0:T(8,128)(2,1)} %get-tuple-element.443, s32[]{:T(128)S(6)} %copy.110), kind=kOutput, calls=%fused_computation.19.clone.1 | convolution fusion | flops 1101004800 | bytes 43024388 | tf_op jit(solution)/shard_map/while/body/eval_jaxpr/hqk,qhe->khe/dot_general | solution.py:169
  541.9 24.2 %multiply_reduce_fusion.8 = (f32[16,512]{1,0:T(8,128)S(1)}, f32[16,512,1024]{2,1,0:T(8,128)}) fusion(f32[16,512,1024]{2,1,0:T(8,128)} %fusion.118, f32[16,512]{1,0:T(8,128)S(1)} %dynamic-slice_bitcast_fusion.2, bf16[1024,16,64]{0,2,1:T(8,128)(2,1)} %get-tuple-element.444, bf16[2,512,16,64]{1,3,2,0:T(8,128)(2,1)} %get-tuple-element.443, s32[]{:T(128)S(6)} %copy.110), kind=kOutput, calls=%fused_computation.13.clone.1 | convolution fusion | flops 1107288064 | bytes 70320128 | tf_op jit(solution)/shard_map/while/body/eval_jaxpr/qhe,khe->hqk/dot_general | solution.py:163
  566.0 27.9 %multiply_convert_fusion.3 = bf16[16,512,1024]{2,1,0:T(8,128)(2,1)} fusion(f32[16,512,1024]{2,1,0:T(8,128)} %get-tuple-element.391, f32[16,512,1024]{2,1,0:T(8,128)} %fusion.118, f32[16,512]{1,0:T(8,128)S(1)} %get-tuple-element.392, f32[16,512]{1,0:T(8,128)S(1)} %dynamic-slice_bitcast_fusion.2), kind=kLoop, calls=%fused_computation.12.clone.1 | loop fusion | flops 41943040 | bytes 83951616 | tf_op jit(solution)/shard_map/while/body/eval_jaxpr/convert_element_type | solution.py:167
  623.2 11.3 fusion.51
  635.3 17.0 %fusion.55 = f32[1024,4096]{1,0:T(8,128)} fusion(bf16[1024,4096]{1,0:T(8,128)(2,1)} %copy-done.58, f32[1024,1024]{0,1:T(8,128)} %copy-done.9, f32[1024]{0:T(1024)S(1)} %copy-done.52, f32[1024]{0:T(1024)S(1)} %copy-done.39, f32[1024]{0:T(1024)S(1)} %copy-done.42, f32[1024]{0:T(1024)S(1)} %copy-done.32), kind=kOutput, calls=%fused_computation.102 | convolution fusion | flops 8595177472 | bytes 29376512 | tf_op jit(solution)/shard_map/sd,sf->df/dot_general | solution.py:125
  653.0 14.2 %multiply_convert_fusion.1 = bf16[1024,4096]{1,0:T(8,128)(2,1)S(1)} fusion(f32[1024,4096]{1,0:T(8,128)} %get-tuple-element.269, f32[1024,4096]{1,0:T(8,128)} %fusion.56, f32[4096]{0:T(1024)S(1)} %bitcast.124), kind=kLoop, calls=%fused_computation.42 | loop fusion | flops 16777216 | bytes 41959424 | tf_op jit(solution)/shard_map/convert_element_type | solution.py:108
  670.5 11.5 fusion.67
  682.7 15.3 %add_convert_fusion.3 = bf16[1024,1024]{0,1:T(8,128)(2,1)} fusion(f32[1024,1024]{0,1:T(8,128)} %copy-done.9, f32[1024]{0:T(1024)S(1)} %convert_element_type.103, bf16[1024,4096]{1,0:T(8,128)(2,1)} %copy-done.14, bf16[4096,1024]{1,0:T(8,128)(2,1)} %all-gather.12.cloned.1.call-done), kind=kOutput, calls=%fused_computation.82 | convolution fusion | flops 8593080320 | bytes 23072768 | tf_op jit(solution)/shard_map/dot_general | solution.py:111
  702.0 12.1 %fusion.64 = (f32[1024]{0:T(1024)S(1)}, f32[1024,1024]{1,0:T(8,128)}) fusion(bf16[1024,3072]{1,0:T(8,128)(2,1)} %all-gather.6.cloned.1.call-done, bf16[1024,1024]{0,1:T(8,128)(2,1)} %bitcast.114, bf16[1024,1024]{0,1:T(8,128)(2,1)} %bitcast.111, bf16[1024,1024]{0,1:T(8,128)(2,1)} %bitcast.117), kind=kOutput, calls=%fused_computation.109 | convolution fusion | flops 6462372864 | bytes 16781312 | tf_op jit(solution)/shard_map/sb,ab->sa/dot_general | solution.py:202
  731.9 40.9 %all-reduce.15 = (f32[1024]{0:T(1024)S(1)}, f32[1024]{0:T(1024)S(1)}, f32[2048]{0:T(1024)S(1)}, f32[1024]{0:T(1024)S(1)}, f32[1024]{0:T(1024)S(1)}, /*index=5*/f...) all-reduce(f32[1024]{0:T(1024)S(1)} %get-tuple-element.220, ...), channel_id=2, replica_groups=mesh['wide'=8,'narrow'=4] {'wide','narrow'}, use_global_device_ids=true, to_apply=%region_16.17.clone | all-reduce | flops 12288 | bytes 98304
  789.0 184.9 %reduce-scatter.9.cloned.1.call-done = f32[32,4096]{1,0:T(8,128)} async-done(((f32[1024,4096]{1,0:T(8,128)}), f32[32,4096]{1,0:T(8,128)}) %reduce-scatter.9.cloned.1.call-update) | async-done | bytes 524304 | tf_op jit(solution)/shard_map/reduce_scatter | solution.py:135
  973.9 187.5 %reduce-scatter.11.cloned.1.call-done = f32[128,1024]{1,0:T(8,128)} async-done(((f32[4096,1024]{1,0:T(8,128)}), f32[128,1024]{1,0:T(8,128)}) %reduce-scatter.11.cloned.1.call-update) | async-done | bytes 524304 | tf_op jit(solution)/shard_map/reduce_scatter | solution.py:137
  (228 shorter events, 184.4 us)
Async XLA Ops:
  7.2 102.8 %all-gather.6.cloned.1.call-start = ((), (), s32[]{:S(2)}) async-start(), calls=%async_computation.4 | async-start | bytes 6488064 | tf_op jit(solution)/shard_map/all_gather | solution.py:51
  7.9 234.0 %all-gather.8.cloned.1.call-start = ((), (), s32[]{:S(2)}) async-start(), calls=%async_computation.5 | async-start | bytes 2162688 | tf_op jit(solution)/shard_map/all_gather | solution.py:53
  8.7 241.5 %all-gather.10.cloned.1.call-start = ((), (), s32[]{:S(2)}) async-start(), calls=%async_computation.6 | async-start | bytes 8650752 | tf_op jit(solution)/shard_map/all_gather | solution.py:97
  9.4 290.1 %all-gather.12.cloned.1.call-start = ((), (), s32[]{:S(2)}) async-start(), calls=%async_computation.7 | async-start | bytes 8650752 | tf_op jit(solution)/shard_map/all_gather | solution.py:99
  10.0 771.5 %reduce-scatter.7.cloned.1.call-start = ((), (), s32[]{:S(2)}) async-start(), calls=%async_computation.9 | async-start | bytes 4325376 | tf_op jit(solution)/shard_map/reduce_scatter | solution.py:214
  59.0 51.0 %copy-start.28 = (f32[1024]{0:T(1024)}, f32[1024]{0:T(1024)S(1)}, u32[]{:S(2)}) copy-start(f32[1024]{0:T(1024)S(1)} %convert_element_type.90) | copy-start | bytes 12292
  59.6 50.4 %copy-start.53 = (f32[1024]{0:T(1024)}, f32[1024]{0:T(1024)S(1)}, u32[]{:S(2)}) copy-start(f32[1024]{0:T(1024)S(1)} %convert_element_type.91) | copy-start | bytes 12292
  104.4 5.6 copy-start.3
  104.8 15.6 %copy-start.24 = (f32[1024]{0:T(1024)}, f32[1024]{0:T(1024)S(1)}, u32[]{:S(2)}) copy-start(f32[1024]{0:T(1024)S(1)} %broadcast_multiply_fusion.1) | copy-start | bytes 12292
  106.0 14.4 %copy-start.35 = (f32[1024]{0:T(1024)}, f32[1024]{0:T(1024)S(1)}, u32[]{:S(2)}) copy-start(f32[1024]{0:T(1024)S(1)} %fusion.49) | copy-start | bytes 12292
  236.1 5.8 copy-start.22
  236.1 5.8 copy-start.4
  236.1 5.8 copy-start.55
  247.0 20.2 %copy-start.30 = (f32[1024]{0:T(1024)}, f32[1024]{0:T(1024)S(1)}, u32[]{:S(2)}) copy-start(f32[1024]{0:T(1024)S(1)} %broadcast_multiply_fusion) | copy-start | bytes 12292
  250.1 17.1 %copy-start.40 = (f32[1024]{0:T(1024)}, f32[1024]{0:T(1024)S(1)}, u32[]{:S(2)}) copy-start(f32[1024]{0:T(1024)S(1)} %fusion.50) | copy-start | bytes 12292
  250.1 49.4 %copy-start.19 = (bf16[1024,1024]{1,0:T(8,128)(2,1)S(1)}, bf16[1024,1024]{1,0:T(8,128)(2,1)}, u32[]{:S(2)}) copy-start(bf16[1024,1024]{1,0:T(8,128)(2,1)} %param.31) | copy-start | bytes 6291460
  250.1 49.4 %copy-start.26 = (f32[32,1,128]{2,1,0:T(1,128)S(1)}, f32[32,1,128]{2,1,0:T(1,128)}, u32[]{:S(2)}) copy-start(f32[32,1,128]{2,1,0:T(1,128)} %convert_element_type.113) | copy-start | bytes 49156
  299.5 51.7 %copy-start.57 = (bf16[1024,4096]{1,0:T(8,128)(2,1)S(1)}, bf16[1024,4096]{1,0:T(8,128)(2,1)}, u32[]{:S(2)}) copy-start(bf16[1024,4096]{1,0:T(8,128)(2,1)} %all-gather.10.cloned.1.call-done) | copy-start | bytes 25165828
  351.2 11.1 copy-start.58
  362.3 5.5 copy-start.31
  362.3 5.5 copy-start.38
  362.3 5.6 copy-start.41
  367.9 5.4 copy-start.46
  367.9 5.4 copy-start.10
  367.9 5.9 copy-start.11
  382.4 406.6 %reduce-scatter.5.cloned.1.call-start = ((), (), s32[]{:S(2)}) async-start(), calls=%async_computation.8 | async-start | bytes 12976128 | tf_op jit(solution)/shard_map/reduce_scatter | solution.py:212
  394.1 7.1 copy-start.23
  488.3 11.7 copy-start
  593.9 11.5 copy-start
  634.6 339.3 %reduce-scatter.9.cloned.1.call-start = ((), (), s32[]{:S(2)}) async-start(), calls=%async_computation.10 | async-start | bytes 17301504 | tf_op jit(solution)/shard_map/reduce_scatter | solution.py:135
  652.3 509.2 %reduce-scatter.11.cloned.1.call-start = ((), (), s32[]{:S(2)}) async-start(), calls=%async_computation.11 | async-start | bytes 17301504 | tf_op jit(solution)/shard_map/reduce_scatter | solution.py:137
  653.0 17.5 %copy-start.20 = (bf16[1024,1024]{1,0:T(8,128)(2,1)S(1)}, bf16[1024,1024]{1,0:T(8,128)(2,1)}, u32[]{:S(2)}) copy-start(bf16[1024,1024]{1,0:T(8,128)(2,1)} %param.31) | copy-start | bytes 6291460
  (36 other events, 96.7 us)
Sparse Core Ops, SparseCore 0:
  10.9 72.4 all-gather.5
  86.3 54.8 all-gather.7
  144.1 76.4 all-gather.9
  223.3 76.1 all-gather.11
  382.5 139.9 reduce-scatter.6
  634.7 154.1 reduce-scatter.4
  791.9 181.9 reduce-scatter.8
  976.9 184.5 reduce-scatter.10
where the time goes:
time: 1180 us; the launch traced here: 1170 us
  waiting for transfers between devices  415 us (35%)
  matrix products  390 us (33%)
  blocking collectives  124 us (11%)
  other arithmetic  122 us (10%)
  local copies, waits for them, and re-layouts  101 us (9%)
  between operations  15.3 us (1%)
    reduce_scatter x1, waiting for transfers between devices, local(): lax.psum_scatter(grad_down_weight, ('wide', 'narrow'), scatter_dimension=...  188 us
    reduce_scatter x1, waiting for transfers between devices, local(): lax.psum_scatter(grad_up_weight, ('wide', 'narrow'), scatter_dimension=0,...  185 us
    unnamed x2, blocking collectives  83.4 us
    convert_element_type x2, other arithmetic, back_block(): grad_scores = (attn_probs * (grad_probs - row_delta)).astype(jnp.bfloat16)  56 us
    dot_general x1, matrix products, local(): jnp.einsum('sd,fd->sf', cotangent, down_back, preferred_element_type=jnp....  51.7 us
    unnamed x146, local copies, waits for them, and re-layouts  50.8 us
    dot_general x2, matrix products, back_block(): jnp.einsum('qhe,khe->hqk', grad_block, value_rows, preferred_element_type...  48.5 us
    all_gather x1, blocking collectives, local(): lax.all_gather(up_bias, ('wide', 'narrow'), axis=0, tiled=True)  40.7 us
  transfers between devices with their start and end apart: 8, of which 4 were waited for; matrix products, arithmetic and copies ran while one was open for 44% of the time, Pallas kernels for 0%

commit v1 on v0

--- a/solution.py
+++ b/solution.py
@@ -1,13 +1,747 @@
+import functools
 import jax
 import jax.numpy as jnp
 from jax import lax
+from jax.experimental import pallas as pl
+from jax.experimental.pallas import tpu as pltpu
 from jax.sharding import PartitionSpec as P
 
 H = 16
 HD = 64
-
-
 epsilon = 1e-05
+bf16 = jnp.bfloat16
+f32 = jnp.float32
+NN = (((1,), (0,)), ((), ()))
+NT = (((1,), (1,)), ((), ()))
+TN = (((0,), (0,)), ((), ()))
+ALL = slice(None)
+MESH = pl.DeviceIdType.MESH
+HBM = pl.BlockSpec(memory_space=pltpu.HBM)
+
+ORDERS = ((0, 2, 1, 3), (0, 3, 1, 2))
+PIECES = 12
+LAG_F = 2
+LAG_B = 1
+
+
+def dot(a, b, dims):
+    return lax.dot_general(a, b, dims, preferred_element_type=f32)
+
+
+def device_bits():
+    w = lax.axis_index("wide")
+    n = lax.axis_index("narrow")
+    return (w // 4, (w // 2) % 2, w % 2, n // 2, n % 2)
+
+
+def flipped(b, dim):
+    t = tuple(1 - v if i == dim else v for i, v in enumerate(b))
+    return (t[0] * 4 + t[1] * 2 + t[2], t[3] * 2 + t[4])
+
+
+def enter(b):
+    barrier = pltpu.get_barrier_semaphore()
+    for dim in range(5):
+        pl.semaphore_signal(barrier, inc=1, device_id=flipped(b, dim), device_id_type=MESH)
+    return lambda: pl.semaphore_wait(barrier, 5)
+
+
+def head_mask(head, rows):
+    return lax.shift_right_logical(lax.broadcasted_iota(jnp.int32, (rows, 256), 1), 6) == head
+
+
+def norm_stats(v):
+    mean = jnp.mean(v, axis=1, keepdims=True)
+    centred = v - mean
+    rstd = lax.rsqrt(jnp.mean(centred * centred, axis=1, keepdims=True) + epsilon)
+    return centred, rstd
+
+
+def quarter(kind, group):
+    return group + (0, 2, 4)[kind] if group < 2 else group + (4, 6, 8)[kind]
+
+
+def forward_kernel(
+    tok_h, vec_h, qkv_h, out_h, up_h, down_h,
+    gw, rows_o, upb_o, actt_o, proj_o, mixt_o, lse_o, hid_o, actb_o, actbt_o,
+    gv, tok, act, wbuf, proj, mixed, trans, oacc, lse, hid, rows, upb,
+    lsem, ssem, rsem, vssem, vrsem, osem, wsem,
+):
+    b = device_bits()
+    ready = enter(b)
+    sources = [
+        [(qkv_h.at[:, 0:512], 0), (qkv_h.at[:, 1024:1536], 512)],
+        [(qkv_h.at[:, 2048:2560], 0), (qkv_h.at[:, 512:1024], 512)],
+        [(qkv_h.at[:, 1536:2048], 0), (qkv_h.at[:, 2560:3072], 512)],
+        [(out_h, None)],
+    ]
+    sources += [[(down_h.at[pl.ds(32 * i, 32)], None)] for i in range(4)]
+    sources += [[(up_h.at[:, pl.ds(1024 * i, 1024)], None)] for i in range(4)]
+    vec_in = pltpu.make_async_copy(vec_h, gv.at[b], lsem.at[0])
+    vec_in.start()
+    tok_in = pltpu.make_async_copy(tok_h, tok, lsem.at[1])
+    own, k = [], 2
+    for p in range(PIECES):
+        own.append([])
+        for src, col in sources[p]:
+            dst = gw.at[(p,) + b] if col is None else gw.at[(p,) + b + (ALL, pl.ds(col, 512))]
+            cp = pltpu.make_async_copy(src, dst, lsem.at[k])
+            cp.start()
+            own[p].append(cp)
+            k += 1
+    tok_in.start()
+    ready()
+    pend = {}
+
+    def send(p, dim, sub, s):
+        cp = pltpu.make_async_remote_copy(
+            src_ref=gw.at[(p,) + sub], dst_ref=gw.at[(p,) + sub], send_sem=ssem.at[p, s], recv_sem=rsem.at[p, s],
+            device_id=flipped(b, dim), device_id_type=MESH)
+        cp.start()
+        pend[(p, s)] = cp
+
+    def stage(p, r):
+        if r == 0:
+            for cp in own[p]:
+                cp.wait()
+        for h in range(2):
+            order = ORDERS[h]
+            cols = (ALL, pl.ds(h * 512, 512))
+            if r > 0:
+                pend[(p, h * 6 + r - 1)].wait_recv()
+            sub = tuple(ALL if i in order[:r] else b[i] for i in range(5)) + cols
+            if r < 4:
+                send(p, order[r], sub, h * 6 + r)
+            if r == 3:
+                send(p, 4, sub, h * 6 + 4)
+            if r == 4:
+                last = tuple(ALL if i in order[:3] else (1 - b[i] if i == order[3] else b[i]) for i in range(5))
+                send(p, 4, last + cols, h * 6 + 5)
+
+    def tick(t):
+        for r in range(4, -1, -1):
+            if 0 <= t - r * LAG_F < PIECES:
+                stage(t - r * LAG_F, r)
+
+    def arrive(p):
+        for s in (4, 5, 10, 11):
+            pend[(p, s)].wait_recv()
+
+    vec_order = (0, 2, 1, 3, 4)
+    vpend = []
+
+    def vec_round(r):
+        if r == 0:
+            vec_in.wait()
+        else:
+            vpend[r - 1].wait_recv()
+        if r < 5:
+            sub = tuple(ALL if i in vec_order[:r] else b[i] for i in range(5))
+            cp = pltpu.make_async_remote_copy(
+                src_ref=gv.at[sub], dst_ref=gv.at[sub], send_sem=vssem.at[r], recv_sem=vrsem.at[r],
+                device_id=flipped(b, vec_order[r]), device_id_type=MESH)
+            cp.start()
+            vpend.append(cp)
+
+    outs = []
+
+    def put(src, dst):
+        cp = pltpu.make_async_copy(src, dst, osem.at[len(outs)])
+        cp.start()
+        outs.append(cp)
+
+    for t in range(6):
+        tick(t)
+        vec_round(t)
+
+    table = gv[...].reshape(32, 8, 128)
+    sub_index = lax.broadcasted_iota(jnp.int32, (32, 8, 128), 1)
+    lines = [jnp.sum(jnp.where(sub_index == r, table, 0.0), axis=1) for r in range(3)]
+
+    def spread(line, offset, log, base):
+        j = lax.broadcasted_iota(jnp.int32, (128, 1024), 0)
+        n = lax.broadcasted_iota(jnp.int32, (128, 1024), 1)
+        pick = jnp.where(j == offset + (n & ((1 << log) - 1)), 1.0, 0.0).astype(bf16)
+        wide = dot(line.astype(bf16), pick, NN)
+        d = lax.broadcasted_iota(jnp.int32, (32, 1024), 0)
+        n = lax.broadcasted_iota(jnp.int32, (32, 1024), 1)
+        return jnp.sum(jnp.where(d == base + lax.shift_right_logical(n, log), wide, 0.0), axis=0, keepdims=True)
+
+    places = ((0, 0, 5, 0), (0, 32, 5, 0), (0, 64, 5, 0), (0, 96, 5, 0), (1, 0, 5, 0), (1, 32, 5, 0), (1, 64, 6, 0), (1, 64, 6, 16))
+    for i, (line, offset, log, base) in enumerate(places):
+        rows[i : i + 1, :] = spread(lines[line], offset, log, base)
+    for d in range(32):
+        upb[d // 4, :, (d % 4) * 128 : (d % 4) * 128 + 128] = jnp.broadcast_to(lines[2][d : d + 1, :], (8, 128))
+    put(rows, rows_o)
+    put(upb, upb_o)
+
+    tok_in.wait()
+    for i in range(4):
+        r = pl.ds(256 * i, 256)
+        centred, rstd = norm_stats(tok[r, :].astype(f32))
+        a = (centred * rstd * rows[0:1, :] + rows[1:2, :]).astype(bf16)
+        act[r, :] = a
+        trans[0, :, r] = a.T
+    put(trans.at[0], actt_o)
+
+    def load_weight(p, slot):
+        arrive(p)
+        cp = pltpu.make_async_copy(gw.at[p], wbuf.at[slot], wsem.at[slot])
+        cp.start()
+        cp.wait()
+
+    def project(p, slot):
+        zero = jnp.zeros((1, 512), f32)
+        q_lo, q_hi, v_lo, v_hi = rows[6:7, 0:512], rows[6:7, 512:1024], rows[7:8, 0:512], rows[7:8, 512:1024]
+        bias = jnp.concatenate(((q_lo, zero), (v_lo, q_hi), (zero, v_hi))[p], axis=1)
+
+        def block(i, carry):
+            r = pl.ds(pl.multiple_of(i * 256, 256), 256)
+            x = (dot(act[r, :], wbuf[slot].reshape(1024, 1024), NN) + bias).astype(bf16)
+            for j in range(4):
+                proj[4 * p + j, r, :] = x[:, 256 * j : 256 * j + 256]
+            return carry
+
+        lax.fori_loop(0, 4, block, 0)
+
+    def attend(group, first):
+        q, k, v = (proj.at[quarter(kind, group)] for kind in range(3))
+
+        def one(i, carry):
+            head = first + i
+            mask = head_mask(head, 1024)
+            vm = jnp.where(mask, v[...], bf16(0))
+            lane = lax.broadcasted_iota(jnp.int32, (512, 128), 1)
+            for j in range(2):
+                r = pl.ds(512 * j, 512)
+                qm = jnp.where(mask[:512], q[r, :], bf16(0)) * bf16(0.125)
+                s = dot(qm, k[...], NT)
+                m = jnp.max(s, axis=1, keepdims=True)
+                p = jnp.exp(s - m)
+                total = jnp.sum(p, axis=1, keepdims=True)
+                o = dot(p.astype(bf16), vm, NN) * (1.0 / total)
+                oacc[r, :] = jnp.where(mask[:512], o, oacc[r, :])
+                lse[r, :] = jnp.where(lane == group * 4 + head, m + jnp.log(total), lse[r, :])
+            return carry
+
+        lax.fori_loop(0, 2, one, 0)
+
+    lse[...] = jnp.zeros_like(lse)
+    t = 6
+    for t in range(6, 10):
+        tick(t)
+    load_weight(0, 0)
+    project(0, 0)
+    tick(10)
+    load_weight(1, 1)
+    project(1, 1)
+    t = 11
+    for group in range(4):
+        if group == 2:
+            load_weight(2, 0)
+            project(2, 0)
+        for first in (0, 2):
+            attend(group, first)
+            tick(t)
+            t += 1
+        mixed[:, 256 * group : 256 * group + 256] = oacc[...].astype(bf16)
+    put(proj, proj_o)
+    put(lse, lse_o)
+    load_weight(3, 1)
+    outs[2].wait()
+    for i in range(4):
+        r = pl.ds(256 * i, 256)
+        v = tok[r, :].astype(f32) + dot(mixed[r, :], wbuf[1].reshape(1024, 1024), NN) + rows[2:3, :]
+        hid[r, :] = v
+        centred, rstd = norm_stats(v)
+        a = (centred * rstd * rows[3:4, :] + rows[4:5, :]).astype(bf16)
+        act[r, :] = a
+        trans[0, :, r] = a.T
+        trans[1, :, r] = mixed[r, :].T
+    put(hid, hid_o)
+    put(act, actb_o)
+    put(trans.at[0], actbt_o)
+    put(trans.at[1], mixt_o)
+    while t < PIECES + 4 * LAG_F:
+        tick(t)
+        t += 1
+    for p in range(4, PIECES):
+        arrive(p)
+    for cp in pend.values():
+        cp.wait_send()
+    for cp in vpend:
+        cp.wait_send()
+    for i, cp in enumerate(outs):
+        if i != 2:
+            cp.wait()
+
+
+def forward_call(tok, vec, qkv, out, up, down):
+    S = jax.ShapeDtypeStruct
+    sem = pltpu.SemaphoreType.DMA
+    big = (2, 2, 2, 2, 2, 32, 1024)
+    return pl.pallas_call(
+        forward_kernel,
+        out_shape=(
+            S((PIECES,) + big, bf16), S((16, 1024), f32), S((8, 8, 512), f32), S((1024, 1024), bf16), S((12, 1024, 256), bf16),
+            S((1024, 1024), bf16), S((1024, 128), f32), S((1024, 1024), f32), S((1024, 1024), bf16), S((1024, 1024), bf16)),
+        in_specs=[HBM] * 6,
+        out_specs=(HBM,) * 10,
+        scratch_shapes=[
+            pltpu.VMEM((2, 2, 2, 2, 2, 8, 128), f32), pltpu.VMEM((1024, 1024), bf16), pltpu.VMEM((1024, 1024), bf16),
+            pltpu.VMEM((2,) + big, bf16), pltpu.VMEM((12, 1024, 256), bf16), pltpu.VMEM((1024, 1024), bf16),
+            pltpu.VMEM((2, 1024, 1024), bf16), pltpu.VMEM((1024, 256), f32), pltpu.VMEM((1024, 128), f32),
+            pltpu.VMEM((1024, 1024), f32), pltpu.VMEM((16, 1024), f32), pltpu.VMEM((8, 8, 512), f32),
+            sem((17,)), sem((PIECES, 12)), sem((PIECES, 12)), sem((5,)), sem((5,)), sem((10,)), sem((2,))],
+        compiler_params=pltpu.CompilerParams(collective_id=1, has_side_effects=True, vmem_limit_bytes=60 << 20),
+        name="forward",
+    )(tok, vec, qkv, out, up, down)
+
+
+def mlp_kernel(actb, actbt, cot, hid, rows, upb, up_w, down_w, out_o, ghid_o, gbr_o, vr_o, ggd_o, ggu_o, total, gab, actc, gpre, down):
+    j = pl.program_id(0)
+
+    @pl.when(j == 0)
+    def _():
+        total[...] = jnp.zeros_like(total)
+        gab[...] = jnp.zeros_like(gab)
+
+    for d in range(4):
+        for i in range(4):
+            down[pl.ds(128 * d + 32 * i, 32), :] = down_w[i, d]
+    bias_sum = jnp.zeros((1, 512), f32)
+    for i in range(4):
+        r = pl.ds(256 * i, 256)
+        up = up_w[0].reshape(1024, 512)
+        v = dot(actb[r, :], up, NN) + upb[0, 0:1, :]
+        back = dot(cot[r, :], down[...], NT)
+        cdf = 0.5 * (1.0 + lax.erf(v * 0.7071067811865476))
+        slope = cdf + v * jnp.exp(-0.5 * v * v) * 0.3989422804014327
+        c = (v * cdf).astype(bf16)
+        g = (back * slope).astype(bf16)
+        actc[r, :] = c
+        gpre[r, :] = g
+        bias_sum = bias_sum + jnp.sum(g.astype(f32), axis=0, keepdims=True)
+        total[r, :] += dot(c, down[...], NN)
+        gab[r, :] += dot(g, up, NT)
+    vr_o[pl.ds(4 + j // 2, 1), pl.ds(pl.multiple_of((j % 2) * 512, 512), 512)] = bias_sum
+    gd = dot(actc[...], cot[...], TN).astype(bf16)
+    for d in range(4):
+        for i in range(4):
+            ggd_o[i, d] = gd[128 * d + 32 * i : 128 * d + 32 * i + 32]
+    ggu_o[...] = dot(actbt[...], gpre[...], NN).astype(bf16).reshape(1, 32, 32, 512)
+
+    @pl.when(j == pl.num_programs(0) - 1)
+    def _():
+        sums = [jnp.zeros((1, 1024), f32)] * 4
+        for i in range(4):
+            r = pl.ds(256 * i, 256)
+            h = hid[r, :]
+            out_o[r, :] = (h + total[r, :] + rows[5:6, :]).astype(bf16)
+            centred, rstd = norm_stats(h)
+            xhat = centred * rstd
+            e = gab[r, :]
+            eg = e * rows[3:4, :]
+            back = rstd * (eg - jnp.mean(eg, axis=1, keepdims=True) - xhat * jnp.mean(eg * xhat, axis=1, keepdims=True))
+            y = cot[r, :].astype(f32)
+            gh = y + back
+            ghid_o[r, :] = gh
+            gb = gh.astype(bf16)
+            gbr_o[r, :] = gb
+            parts = (e * xhat, e, y, gb.astype(f32))
+            sums = [s + jnp.sum(x, axis=0, keepdims=True) for s, x in zip(sums, parts)]
+        for i in range(4):
+            vr_o[i : i + 1, :] = sums[i]
+
+
+def mlp_call(actb, actbt, cot, hid, rows, upb, gw):
+    S = jax.ShapeDtypeStruct
+    once = lambda shape: pl.BlockSpec(shape, lambda j: (0,) * len(shape), pipeline_mode=pl.Buffered(1))
+    return pl.pallas_call(
+        mlp_kernel,
+        grid=(8,),
+        out_shape=(
+            S((1024, 1024), bf16), S((1024, 1024), f32), S((1024, 1024), bf16), S((8, 1024), f32),
+            S((4, 32, 32, 1024), bf16), S((4, 32, 32, 1024), bf16)),
+        in_specs=[
+            once((1024, 1024)), once((1024, 1024)), once((1024, 1024)), once((1024, 1024)), once((16, 1024)),
+            pl.BlockSpec((1, 8, 512), lambda j: (j, 0, 0)),
+            pl.BlockSpec((1, 32, 32, 512), lambda j: (8 + j // 2, 0, 0, j % 2)),
+            pl.BlockSpec((4, 4, 32, 1024), lambda j: (1, j, 0, 0))],
+        out_specs=(
+            pl.BlockSpec((1024, 1024), lambda j: (0, 0)), pl.BlockSpec((1024, 1024), lambda j: (0, 0)),
+            pl.BlockSpec((1024, 1024), lambda j: (0, 0)), pl.BlockSpec((8, 1024), lambda j: (0, 0)),
+            pl.BlockSpec((4, 4, 32, 1024), lambda j: (0, j, 0, 0)),
+            pl.BlockSpec((1, 32, 32, 512), lambda j: (j // 2, 0, 0, j % 2))),
+        scratch_shapes=[
+            pltpu.VMEM((1024, 1024), f32), pltpu.VMEM((1024, 1024), f32), pltpu.VMEM((1024, 512), bf16),
+            pltpu.VMEM((1024, 512), bf16), pltpu.VMEM((512, 1024), bf16)],
+        compiler_params=pltpu.CompilerParams(vmem_limit_bytes=60 << 20),
+        name="mlp",
+    )(actb, actbt, cot, hid, rows, upb, gw, gw)
+
+
+RC = 4
+AC = 4
+
+
+def backward_kernel(
+    proj_h, actt_h, mixt_h, lse_h, gbr_h, ghid_h, tok_h, gw, ggd, ggu, rows_h, vr_h,
+    gtok_o, gqkv_o, gout_o, gup_o, gdown_o, vec_o,
+    acc, rc, r1, r2, r3, r4, fin, stag, dout, gp, qkv, tok, wide, actt, w, gaa, lse, rows, vsum, vrecv,
+    lsem, accsem, ssem, rsem, credit, vssem, vrsem, fsem,
+):
+    b = device_bits()
+    zh, zl, x, y, c = b
+    ready = enter(b)
+    loads = []
+
+    def load(src, dst):
+        cp = pltpu.make_async_copy(src, dst, lsem.at[len(loads)])
+        cp.start()
+        loads.append(cp)
+        return cp
+
+    rows_in = load(rows_h, rows)
+    vr_in = load(vr_h, vsum.at[pl.ds(0, 8)])
+    lse_in = load(lse_h, lse)
+    gbr_in = load(gbr_h, tok)
+    mixt_in = load(mixt_h, actt)
+    ready()
+    pend = {}
+    fins = []
+
+    def source(p):
+        if p == 1:
+            return stag.at[0]
+        if p < 5:
+            return ggd.at[max(p - 1, 0)]
+        if p < 9:
+            return ggu.at[p - 5]
+        return stag.at[p % 2]
+
+    def send(p, s, dim, src, dst):
+        cp = pltpu.make_async_remote_copy(
+            src_ref=src, dst_ref=dst, send_sem=ssem.at[p, s], recv_sem=rsem.at[p, s], device_id=flipped(b, dim), device_id_type=MESH)
+        cp.start()
+        pend[(p, s)] = cp
+
+    def sent(p, s):
+        pend[(p, s)].wait_send()
+        pend.pop((p, s))
+
+    recv = {}
+
+    def got(p, s):
+        recv[(p, s)].wait_recv()
+
+    def final_places(p):
+        if p == 1:
+            return [(gout_o, 0, 1024)]
+        if p < 5:
+            return [(gdown_o.at[pl.ds(32 * max(p - 1, 0), 32)], 0, 1024)]
+        if p < 9:
+            return [(gup_o.at[:, pl.ds(1024 * (p - 5), 1024)], 0, 1024)]
+        first, second = ((0, 1024), (2048, 512), (1536, 2560))[p - 9]
+        return [(gqkv_o.at[:, pl.ds(first, 512)], 0, 512), (gqkv_o.at[:, pl.ds(second, 512)], 512, 512)]
+
+    half = (pl.ds(0, 512), pl.ds(512, 512))
+
+    def stage(p, r):
+        a = acc.at[p % AC]
+        if r == 0:
+            if p >= RC:
+                pl.semaphore_wait(credit, 1)
+            if p >= AC:
+                sent(p - AC, 1)
+                sent(p - AC, 2)
+            send(p, 0, 4, source(p).at[:, :, :, :, 1 - c], rc.at[p % RC])
+            recv[(p, 0)] = pend[(p, 0)]
+            cp = pltpu.make_async_copy(source(p).at[:, :, :, :, c], a, accsem.at[p])
+            cp.start()
+            recv[(p, "own")] = cp
+        if r == 1:
+            got(p, 0)
+            recv[(p, "own")].wait()
+            in_slot = rc.at[p % RC]
+
+            def add(i, carry):
+                k = (i // 8, (i // 4) % 2, (i // 2) % 2, i % 2)
+                a[k] = a[k] + in_slot[k]
+                return carry
+
+            lax.fori_loop(0, 16, add, 0)
+            if p + RC < PIECES:
+                pl.semaphore_signal(credit, inc=1, device_id=flipped(b, 4), device_id_type=MESH)
+            send(p, 1, 3, a.at[:, :, :, 1 - y, :, half[0]], r1.at[p, 0])
+            send(p, 2, 2, a.at[:, :, 1 - x, :, :, half[1]], r1.at[p, 1])
+            recv[(p, 1)], recv[(p, 2)] = pend[(p, 1)], pend[(p, 2)]
+        if r == 2:
+            for h in range(2):
+                got(p, 1 + h)
+
+                def add(i, carry, h=h):
+                    k = (i // 4, (i // 2) % 2, i % 2)
+                    full = (k[0], k[1], k[2], y) if h == 0 else (k[0], k[1], x, k[2])
+                    r1[(p, h) + k] = r1[(p, h) + k] + a[full + (ALL, half[h])]
+                    return carry
+
+                lax.fori_loop(0, 8, add, 0)
+                send(p, 3 + h, 1, r1.at[p, h, :, 1 - zl], r2.at[p, h])
+                recv[(p, 3 + h)] = pend[(p, 3 + h)]
+        if r == 3:
+            for h in range(2):
+                got(p, 3 + h)
+                for i in range(2):
+                    for j in range(2):
+                        r2[p, h, i, j] = r2[p, h, i, j] + r1[p, h, i, zl, j]
+                mine = (x, y)[h]
+                send(p, 5 + h, 2 + h, r2.at[p, h, :, 1 - mine], r3.at[p, h])
+                recv[(p, 5 + h)] = pend[(p, 5 + h)]
+        if r == 4:
+            for h in range(2):
+                got(p, 5 + h)
+                mine = (x, y)[h]
+                for i in range(2):
+                    r3[p, h, i] = r3[p, h, i] + r2[p, h, i, mine]
+                send(p, 7 + h, 0, r3.at[p, h, 1 - zh], r4.at[p, h])
+                recv[(p, 7 + h)] = pend[(p, 7 + h)]
+        if r == 5:
+            for h in range(2):
+                got(p, 7 + h)
+                fin[p, :, half[h]] = r3[p, h, zh].astype(f32) + r4[p, h].astype(f32)
+            for dst, col, width in final_places(p):
+                cp = pltpu.make_async_copy(fin.at[p, :, pl.ds(col, width)], dst, fsem.at[len(fins)])
+                cp.start()
+                fins.append(cp)
+
+    issued = {}
+    clock = [0]
+
+    def tick(limit):
+        for r in range(5, -1, -1):
+            for p in range(PIECES):
+                if issued.get((p, r)):
+                    continue
+                if r == 0:
+                    if p < limit and (p == 0 or issued.get((p - 1, 0))) and not issued.get(("at", clock[0])):
+                        stage(p, 0)
+                        issued[(p, 0)] = clock[0] + 1
+                        issued[("at", clock[0])] = True
+                elif issued.get((p, r - 1)) and issued[(p, r - 1)] + LAG_B <= clock[0] + 1:
+                    stage(p, r)
+                    issued[(p, r)] = clock[0] + 1
+        clock[0] += 1
+
+    tick(1)
+
+    def stage_store(slot, value, col):
+        for i in range(4):
+            stag[slot, i // 2, i % 2, :, :, :, :, pl.ds(col, 512)] = value(i).astype(bf16).reshape(2, 2, 2, 32, 512)
+
+    def weight(p):
+        cp = load(gw.at[p], w)
+        return cp
+
+    w_in = weight(3)
+    gbr_in.wait()
+    w_in.wait()
+    for i in range(4):
+        r = pl.ds(256 * i, 256)
+        dout[r, :] = dot(tok[r, :], w[...].reshape(1024, 1024), NT).astype(bf16)
+    mixt_in.wait()
+    for col in (0, 512):
+        stage_store(0, lambda i: dot(actt[pl.ds(256 * i, 256), :], tok[:, pl.ds(col, 512)], NN), col)
+    actt_in = load(actt_h, actt)
+    tok_in = load(tok_h, tok)
+    tick(9)
+    vr_in.wait()
+    lse_in.wait()
+
+    def half_piece(kind, upper):
+        where = quarter(kind, 2 * upper)
+        p, col = where // 4, (where % 4) * 256
+        piece = 9 + p
+        slot = piece % 2
+        stage_store(slot, lambda i: dot(actt[pl.ds(256 * i, 256), :], gp[kind], NN), col)
+        if kind != 1:
+            vsum[8 + kind // 2 : 9 + kind // 2, pl.ds(512 * upper, 512)] = jnp.sum(gp[kind].astype(f32), axis=0, keepdims=True)
+        for i in range(4):
+            r = pl.ds(256 * i, 256)
+            part = dot(gp[kind, r, :], w[:, :, :, :, :, :, pl.ds(col, 512)].reshape(1024, 512), NT)
+            if kind == 0 and upper == 0:
+                gaa[r, :] = part
+            else:
+                gaa[r, :] += part
+
+    def attention_phase():
+        dq, dk, dv = (wide.at[:, pl.ds(256 * i, 256)] for i in range(3))
+
+        def fetch(group):
+            return [load(proj_h.at[quarter(kind, group)], qkv.at[group % 2, kind]) for kind in range(3)]
+
+        def back(group, first):
+            q, k, v = (qkv.at[group % 2, kind] for kind in range(3))
+            cols = pl.ds(256 * group, 256)
+
+            def one(i, carry):
+                head = first + i
+                mask = head_mask(head, 1024)
+                some = mask[:512]
+                km = jnp.where(mask, k[...], bf16(0))
+                lane = lax.broadcasted_iota(jnp.int32, (512, 128), 1)
+                dkh, dvh = 0.0, 0.0
+                for j in range(2):
+                    r = pl.ds(512 * j, 512)
+                    qm = jnp.where(some, q[r, :], bf16(0)) * bf16(0.125)
+                    dom = jnp.where(some, dout[r, cols], bf16(0))
+                    level = jnp.sum(jnp.where(lane == group * 4 + head, lse[r, :], 0.0), axis=1, keepdims=True)
+                    p = jnp.exp(dot(qm, k[...], NT) - level)
+                    dp = dot(dom, v[...], NT)
+                    delta = jnp.sum(p * dp, axis=1, keepdims=True)
+                    ds = (p * (dp - delta)).astype(bf16)
+                    dvh = dvh + dot(p.astype(bf16), dom, TN)
+                    dkh = dkh + dot(ds, qm, TN)
+                    dq[r, :] = jnp.where(some, dot(ds, km, NN) * 0.125, dq[r, :])
+                dk[...] = jnp.where(mask, dkh, dk[...])
+                dv[...] = jnp.where(mask, dvh, dv[...])
+                return carry
+
+            lax.fori_loop(0, 2, one, 0)
+
+        flights = {0: fetch(0)}
+        for group in range(4):
+            if group < 3:
+                flights[group + 1] = fetch(group + 1)
+            for cp in flights[group]:
+                cp.wait()
+            for first in (0, 2):
+                back(group, first)
+                tick(9 if group < 2 else 10)
+            at = pl.ds(256 * (group % 2), 256)
+            for kind, total in enumerate((dq, dk, dv)):
+                gp[kind, :, at] = total[...].astype(bf16)
+            if group % 2 == 1:
+                upper = group // 2
+                if upper == 0:
+                    sent(1, 0)
+                    actt_in.wait()
+                    weight(0).wait()
+                    half_piece(0, 0)
+                    half_piece(1, 0)
+                    tick(10)
+                    weight(1).wait()
+                    half_piece(2, 0)
+                    tick(10)
+                else:
+                    ghid_in = load(ghid_h, wide)
+                    half_piece(0, 1)
+                    tick(11)
+                    weight(2).wait()
+                    sent(9, 0)
+                    assert issued[(9, 1)]
+                    half_piece(1, 1)
+                    half_piece(2, 1)
+                    tick(12)
+
+        return ghid_in
+
+    ghid_in = attention_phase()
+
+    def last_phase():
+        rows_in.wait()
+        ghid_in.wait()
+        tok_in.wait()
+        sums = [jnp.zeros((1, 1024), f32)] * 2
+        for i in range(4):
+            r = pl.ds(256 * i, 256)
+            centred, rstd = norm_stats(tok[r, :].astype(f32))
+            xhat = centred * rstd
+            e = gaa[r, :]
+            eg = e * rows[0:1, :]
+            back = rstd * (eg - jnp.mean(eg, axis=1, keepdims=True) - xhat * jnp.mean(eg * xhat, axis=1, keepdims=True))
+            tok[r, :] = (wide[r, :] + back).astype(bf16)
+            sums = [s + jnp.sum(v, axis=0, keepdims=True) for s, v in zip(sums, (e * xhat, e))]
+        tok_out = load(tok, gtok_o)
+        vsum[10:11, :] = sums[0]
+        vsum[11:12, :] = sums[1]
+        vsum[12:16, :] = jnp.zeros((4, 1024), f32)
+        tick(12)
+        for i, dim in enumerate((4, 3, 1, 2, 0)):
+            cp = pltpu.make_async_remote_copy(
+                src_ref=vsum, dst_ref=vrecv.at[i], send_sem=vssem.at[i], recv_sem=vrsem.at[i], device_id=flipped(b, dim),
+                device_id_type=MESH)
+            cp.start()
+            tick(12)
+            cp.wait()
+            vsum[...] = vsum[...] + vrecv[i]
+        own = ((zh * 2 + zl) * 2 + x) * 4 + y * 2 + c
+        n = lax.broadcasted_iota(jnp.int32, (1024, 128), 0)
+        j = lax.broadcasted_iota(jnp.int32, (1024, 128), 1)
+
+        def cut(value, base):
+            pick = jnp.where(n == base + j, 1.0, 0.0)
+            return lax.dot_general(value, pick, NN, precision=lax.Precision.HIGHEST, preferred_element_type=f32)
+
+        narrow = cut(vsum[...], 32 * own)
+        middle = cut(vsum[8:16, :], 64 * (own % 16))
+        broad = cut(vsum[0:8, :], 128 * (own % 8))
+        for i, at in enumerate((10, 11, 3, 0, 1, 2)):
+            vec_o[i : i + 1, :] = narrow[at : at + 1]
+        vec_o[6:7, :] = jnp.where(own < 16, middle[0:1], middle[1:2])
+        up = broad[4:5]
+        for i in range(1, 4):
+            up = jnp.where(own // 8 == i, broad[4 + i : 5 + i], up)
+        vec_o[7:8, :] = up
+        while not issued.get((PIECES - 1, 5)):
+            tick(12)
+        tok_out.wait()
+
+    last_phase()
+    for cp in pend.values():
+        cp.wait_send()
+    for cp in fins:
+        cp.wait()
+
+
+def backward_call(proj, actt, mixt, lse, gbr, ghid, tok, gw, ggd, ggu, rows, vr):
+    S = jax.ShapeDtypeStruct
+    V = pltpu.VMEM
+    sem = pltpu.SemaphoreType.DMA
+    big = (2, 2, 2, 2, 2, 32, 1024)
+    n = PIECES
+    return pl.pallas_call(
+        backward_kernel,
+        out_shape=(
+            S((1024, 1024), bf16), S((32, 3072), f32), S((32, 1024), f32), S((32, 4096), f32), S((128, 1024), f32), S((8, 128), f32)),
+        in_specs=[HBM] * 12,
+        out_specs=(HBM,) * 5 + (pl.BlockSpec(memory_space=pltpu.VMEM),),
+        scratch_shapes=[
+            V((AC, 2, 2, 2, 2, 32, 1024), bf16), V((RC, 2, 2, 2, 2, 32, 1024), bf16), V((n, 2, 2, 2, 2, 32, 512), bf16),
+            V((n, 2, 2, 2, 32, 512), bf16), V((n, 2, 2, 32, 512), bf16), V((n, 2, 32, 512), bf16), V((n, 32, 1024), f32),
+            V((2,) + big, bf16), V((1024, 1024), bf16), V((3, 1024, 512), bf16), V((2, 3, 1024, 256), bf16),
+            V((1024, 1024), bf16), V((1024, 1024), f32), V((1024, 1024), bf16), V(big, bf16),
+            V((1024, 1024), f32), V((1024, 128), f32), V((16, 1024), f32), V((16, 1024), f32), V((5, 16, 1024), f32),
+            sem((40,)), sem((n,)), sem((n, 9)), sem((n, 9)), pltpu.SemaphoreType.REGULAR, sem((5,)), sem((5,)), sem((16,))],
+        compiler_params=pltpu.CompilerParams(collective_id=2, has_side_effects=True, vmem_limit_bytes=63 << 20),
+        name="backward",
+    )(proj, actt, mixt, lse, gbr, ghid, tok, gw, ggd, ggu, rows, vr)
+
+
+def layer(
+    tokens, attn_gain, attn_shift, qkv_weight, qv_bias, out_weight, out_bias, mlp_gain, mlp_shift, up_weight, up_bias, down_weight,
+    down_bias, cotangent,
+):
+    vec = jnp.concatenate([attn_gain, attn_shift, out_bias, mlp_gain, mlp_shift, down_bias, qv_bias, up_bias]).astype(f32)
+    vec = jnp.pad(vec.reshape(3, 128), ((0, 5), (0, 0)))
+    gw, rows, upb, actt, proj, mixt, lse, hid, actb, actbt = forward_call(tokens, vec, qkv_weight, out_weight, up_weight, down_weight)
+    output, ghid, gbr, vr, ggd, ggu = mlp_call(actb, actbt, cotangent, hid, rows, upb, gw.reshape(PIECES, 32, 32, 1024))
+    big = (4, 2, 2, 2, 2, 2, 32, 1024)
+    gtok, gqkv, gout, gup, gdown, gvec = backward_call(
+        proj, actt, mixt, lse, gbr, ghid, tokens, gw, ggd.reshape(big), ggu.reshape(big), rows, vr)
+    return (
+        output, gtok, gvec[0, :32], gvec[1, :32], gqkv, gvec[6, :64], gout, gvec[2, :32], gvec[3, :32], gvec[4, :32], gup, gvec[7],
+        gdown, gvec[5, :32])
 
 
 def layer_norm(values_in, gain_vec, bias_vec):
@@ -27,7 +761,7 @@
     return pull_back(incoming)
 
 
-def local(
+def general_layer(
     tokens,
     attn_gain,
     attn_shift,
@@ -250,7 +984,7 @@
         P(("wide", "narrow"), None),
     )
     return jax.shard_map(
-        local,
+        layer if dict(mesh.shape) == {"wide": 8, "narrow": 4} else general_layer,
         mesh=mesh,
         in_specs=placed,
         out_specs=(

time: 1180 us -> 353 us (0.30)
  waiting for transfers between devices: 415 us -> 0 us
  matrix products: 390 us -> 0 us
  Pallas kernels: 0 us -> 333 us
  blocking collectives: 124 us -> 0 us
  other arithmetic: 122 us -> 0.6 us
  local copies, waits for them, and re-layouts: 101 us -> 15.4 us
  between operations: 15.3 us -> 0.88 us
    dot_general x26 -> x0, matrix products: 390 us -> none  [the longest x1 51.7 us: local(): jnp.einsum('sd,fd->sf', cotangent, down_back, preferred_element_type=jnp....]
    reduce_scatter x4 -> x0, waiting for transfers between devices: 380 us -> none  [the longest x1 188 us: local(): lax.psum_scatter(grad_down_weight, ('wide', 'narrow'), scatter_dimension=...]
    pallas_call x0 -> x3, Pallas kernels: none -> 333 us  [the longest x1 141 us: backward_call(): pl.pallas_call(backward_kernel, out_shape=(S((1024, 1024), bf16), S((32,...]
    unnamed x2 -> x0, blocking collectives: 83.4 us -> none
    convert_element_type x11 -> x0, other arithmetic: 72.6 us -> none  [the longest x2 56 us: back_block(): grad_scores = (attn_probs * (grad_probs - row_delta)).astype(jnp.bfloat16)]
    reduce_sum x12 -> x0, other arithmetic: 49 us -> none  [the longest x2 28.7 us: attend_block(): denominator = jnp.sum(exp_scores, axis=-1, keepdims=True)]
    unnamed x146 -> x13, local copies, waits for them, and re-layouts: 50.8 us -> 6.17 us
    all_gather x1 -> x0, blocking collectives: 40.7 us -> none  [local(): lax.all_gather(up_bias, ('wide', 'narrow'), axis=0, tiled=True)]
  transfers between devices with their start and end apart: 8 -> 0, of which waited for: 4 -> 0; matrix products, arithmetic and copies ran while one was open for 44% -> 0% of each run, Pallas kernels for 0% -> 0%
where the time goes in v1:
time: 353 us; the launch traced here: 350 us
  Pallas kernels  333 us (94%)
  local copies, waits for them, and re-layouts  15.4 us (4%)
    pallas_call x1, Pallas kernels, backward_call(): pl.pallas_call(backward_kernel, out_shape=(S((1024, 1024), bf16), S((32,...  141 us
    pallas_call x1, Pallas kernels, forward_call(): pl.pallas_call(forward_kernel, out_shape=(S((PIECES,) + big, bf16), S((16...  119 us
    pallas_call x1, Pallas kernels, mlp_call(): pl.pallas_call(mlp_kernel, grid=(8,), out_shape=(S((1024, 1024), bf16), S...  72.1 us

profile of v1, /device:TPU:0, one launch (start us, length us, event | category | flops | bytes accessed | tf_op | source)
XLA Modules:
  0.0 349.6 jit_solution(11534545882978068202)
XLA Ops:
  0.6 5.4 %concatenate.3 = bf16[384]{0:T(512)(128)(2,1)S(1)} concatenate(bf16[32]{0:T(256)(128)(2,1)} %param.15, bf16[32]{0:T(256)(128)(2,1)} %param.16, bf16[32]{0:T(256)(128)(2,1)} %param.20, bf16[32]{0:T(256)(128)(2,1)} %param.21, bf16[32]{0:T(256)(128)(2,1)} %param.22, bf16[32]{0:T(256)(128)(2,1)} %param.26, bf16[64]{0:T(256)(128)(2,1)} %param.18, bf16[128]{0:T(256)(128)(2,1)} %param.24), dimensions={0} | concatenate | bytes 1536 | tf_op jit(solution)/shard_map/concatenate | solution.py:735
  6.1 0.6 pad_convert_fusion.vec_h
  6.7 119.1 %forward.1 = (bf16[12,2,2,2,2,2,32,1024]{7,6,5,4,3,2,1,0:T(8,128)(2,1)}, f32[16,1024]{1,0:T(8,128)}, f32[8,8,512]{2,1,0:T(8,128)}, bf16[1024,1024]{1,0:T(8,128)(...) custom-call(bf16[1024,1024]{1,0:T(8,128)(2,1)} %tok_h.3, ...), custom_call_target="tpu_custom_call" | custom-call | tf_op jit(solution)/shard_map/forward/pallas_call | solution.py:283
  125.8 72.1 %mlp.1 = (bf16[1024,1024]{1,0:T(8,128)(2,1)}, f32[1024,1024]{1,0:T(8,128)}, bf16[1024,1024]{1,0:T(8,128)(2,1)}, f32[8,1024]{1,0:T(8,128)}, bf16[4,32,32,1024]{3,...) custom-call(bf16[1024,1024]{1,0:T(8,128)(2,1)} %get-tuple-element.36.actb, bf16[1024,1024]{1,0:T(8,128)(2,1)} %get-tuple-element.37.actbt, ...), custom_call_target="tpu_custom_call" | custom-call | tf_op jit(solution)/shard_map/mlp/pallas_call | solution.py:360
  197.9 141.5 %backward.1 = (bf16[1024,1024]{1,0:T(8,128)(2,1)}, f32[32,3072]{1,0:T(8,128)}, f32[32,1024]{1,0:T(8,128)}, f32[32,4096]{1,0:T(8,128)}, f32[128,1024]{1,0:T(8,128)}, /*index=5*/f32[8,128]{1,0:T(8,128)}) custom-call(bf16[12,1024,256]{2,1,0:T(8,128)(2,1)} %get-tuple-element.43.proj_h, bf16[1024,1024]{1,0:T(8,128)(2,1)} %get-tuple-element.44.actt_h, ...), custom_call_target="tpu_custom_call" | custom-call | tf_op jit(solution)/shard_map/backward/pallas_call | solution.py:713
  339.4 1.2 slice_bitcast_fusion.5
  340.6 1.2 slice_bitcast_fusion.1
  341.8 1.4 slice_bitcast_fusion
  343.2 0.0 copy-start.2
  343.2 0.0 copy-start.3
  343.2 0.0 copy-start.1
  343.2 3.2 copy.33
  346.4 0.0 copy-done.2
  346.4 0.0 copy-start
  346.4 0.7 copy.34
  347.1 0.0 copy-done.3
  347.1 0.7 copy.35
  347.8 0.0 copy-done.1
  347.8 0.8 copy.36
  348.6 0.0 copy-done
  348.6 0.8 copy.37
Async XLA Ops:
  343.2 3.2 copy-start.2
  343.2 3.9 %copy-start.3 = (f32[32,1024]{1,0:T(8,128)S(1)}, f32[32,1024]{1,0:T(8,128)}, u32[]{:S(2)}) copy-start(f32[32,1024]{1,0:T(8,128)} %get-tuple-element.84) | copy-start | bytes 393220
  343.2 4.6 %copy-start.1 = (f32[32,4096]{1,0:T(8,128)S(1)}, f32[32,4096]{1,0:T(8,128)}, u32[]{:S(2)}) copy-start(f32[32,4096]{1,0:T(8,128)} %get-tuple-element.88) | copy-start | bytes 1572868
  346.4 2.2 copy-start
